TPU v7x, 32 devices: a whole 2x2x4 slice. The times are simulated.
32 devices in a mesh: shock: 8 (over z, x), trans: 4 (over y, core).
Axes of the slice: x: 2, y: 2, z: 4, core: 2. Of those that a mesh axis runs over, the one named last changes fastest.
Arguments:
- conserved: float32 [11, 10, 65536], P(None, None, ('shock', 'trans')), may hold values from -6 to 6
- cell_size: float32 [65536], P(('shock', 'trans')), may hold values from 0.5 to 2
- sound_speed: float32 [65536], P(('shock', 'trans')), may hold values from 0.3 to 1.8
- jacobian: float32 [3, 11, 11], replicated, may hold values from -1.75 to 1.75
- derivative: float32 [3, 10, 10], replicated, may hold values from -2 to 2
- restriction: float32 [4, 6, 10], replicated, may hold values from -2 to 2
- lifting: float32 [4, 10, 6], replicated, may hold values from -2.5 to 2.5
- vertex_velocity: float32 [3, 16384], P(None, ('shock', 'trans')), may hold values from -1.8 to 1.8
- share_index: int32 [2, 4096], P(None, ('shock', 'trans')), may hold values from 0 to 511
- elem_vertex: int32 [4, 65536], P(None, ('shock', 'trans')), may hold values from 0 to 767
- inner_elem: int32 [2, 131072], P(None, ('shock', 'trans')), may hold values from 0 to 2047
- inner_face: int32 [2, 131072], P(None, ('shock', 'trans')), may hold values from 0 to 3
- inner_normal: float32 [3, 131072], P(None, ('shock', 'trans')), may hold values from -3 to 3
- slab_elem: int32 [2, 8192], P(None, ('shock', 'trans')), may hold values from 0 to 2047
- slab_face: int32 [2, 8192], P(None, ('shock', 'trans')), may hold values from 0 to 3
- slab_normal: float32 [3, 2, 8192], P(None, None, ('shock', 'trans')), may hold values from -3 to 3
- peer_elem: int32 [4, 2048], P(None, ('shock', 'trans')), may hold values from 0 to 2047
- peer_face: int32 [4, 2048], P(None, ('shock', 'trans')), may hold values from 0 to 3
- peer_normal: float32 [3, 4, 2048], P(None, None, ('shock', 'trans')), may hold values from -3 to 3
- peer_count: int32 [4, 32], P(None, ('shock', 'trans')), may hold values from 0 to 64, as said below
Outputs:
- rate: float32 [11, 10, 65536], P(None, None, ('shock', 'trans'))
- step_size: float32 [], replicated
Inputs may be any that keep to these rules, and one draw needn't show every extreme that they name: peer_count[q, p] is the same for partition p at trans position q' and the partition of the same slab at position q when read from the other side, is 0 for q equal to p's own position, and equals 64 for some pair of each slab; slots at or past it are padding.
All inputs are finite; a program needn't handle non-finite values.
Results may differ from a plain program's by a relative error of at most 0.0003.
Values sent between devices are 32-bit elements; how exact they have to be, the bound alone decides.
A program may use at most 128 MiB of HBM per device.

v0:
```python
import functools

import jax
import jax.numpy as jnp
import numpy as np
from jax import lax
from jax.experimental import pallas as pl
from jax.experimental.pallas import tpu as pltpu
from jax.sharding import PartitionSpec as P

CFL_NUMBER = 0.3
F32 = jnp.float32
BF16 = jnp.bfloat16
MESH = pl.DeviceIdType.MESH
VMEM_BYTES = 56 * 1024 * 1024


def up_to(value, multiple):
    return -(-value // multiple) * multiple


def selections(num_vars, basis, face_basis, faces, rows, trace_rows):
    flat, flat_t = num_vars * basis, num_vars * face_basis
    row, trow = np.arange(rows), np.arange(trace_rows)
    row_v, row_b = np.where(row < flat, row // basis, -1), np.where(row < flat, row % basis, -1)
    trow_v = np.where(trow < flat_t, trow // face_basis, -2)
    trow_f = np.where(trow < flat_t, trow % face_basis, -2)

    def pick(target, count):
        return (target[:, None] == np.arange(count)[None, :]).astype(np.float32)

    def block(target, count, copies):
        out = np.zeros((copies, target.size, copies * count), np.float32)
        for k in range(copies):
            out[k, :, k * count : (k + 1) * count] = pick(target, count)
        return out.reshape(copies * target.size, copies * count)

    same_v = (row_v[:, None] == row_v[None, :]) & (row_v[:, None] >= 0)
    same_tv = (trow_v[:, None] == row_v[None, :]) & (trow_v[:, None] >= 0)
    same_f = (trow_f[:, None] == trow_f[None, :]) & (trow_f[:, None] >= 0)
    keep = np.zeros((trace_rows, rows), np.float32)
    keep[flat_t, flat] = 1.0
    return [
        np.ascontiguousarray(pick(row_v, num_vars).T),
        np.ascontiguousarray(pick(row_b, basis).T),
        block(row_v, num_vars, 3),
        block(row_b, basis, 3),
        block(trow_f, face_basis, faces),
        np.ascontiguousarray(pick(trow_v, num_vars).T),
        block(trow_v, num_vars, 3),
        pick(row_b, basis),
        np.ascontiguousarray(block(trow_f, face_basis, faces).T),
        same_v.astype(np.float32),
        same_tv.astype(np.float32),
        same_f.astype(np.float32),
        np.ascontiguousarray(same_tv.T.astype(np.float32)),
        keep,
    ]


def exact(a, b):
    return jnp.dot(a, b, precision=lax.Precision.HIGHEST, preferred_element_type=F32)


def dot(a, b):
    return jnp.dot(a, b, preferred_element_type=F32)


def split(value):
    high = value.astype(BF16)
    return high, (value - high.astype(F32)).astype(BF16)


def operator(matrix):
    high, low = split(matrix)
    return jnp.concatenate([high, high, low], axis=1)


def operand(value):
    high, low = split(value)
    return jnp.concatenate([high, low, high], axis=0)


def ones_at(index, count):
    places = lax.broadcasted_iota(jnp.int32, (count, index.shape[1]), 0)
    return jnp.where(places == index, 1.0, 0.0).astype(BF16)


def apply_space(space, value, mesh_vel, inverse, rows):
    product = dot(space, operand(value))
    total = product[:rows]
    for d in range(3):
        total = total - mesh_vel[d : d + 1] * product[(d + 1) * rows : (d + 2) * rows]
    return total * inverse


def gather_trace(table, ones, faces, trace_op, rows, trace_rows, num_faces):
    found = dot(table, ones)
    high, low = found[:rows].astype(BF16), found[rows:].astype(BF16)
    every = dot(trace_op, jnp.concatenate([high, low, high], axis=0))
    trace = jnp.where(faces == 0, every[:trace_rows], 0.0)
    for k in range(1, num_faces):
        trace = trace + jnp.where(faces == k, every[k * trace_rows : (k + 1) * trace_rows], 0.0)
    return trace


def front_kernel(
    sizes,
    conserved_ref,
    scalars_ref,
    vertex_ref,
    share_ref,
    corner_ref,
    jac_ref,
    der_ref,
    res_ref,
    lift_ref,
    bound_index_ref,
    sel_vt,
    sel_bt,
    sel_jac,
    sel_der,
    sel_res,
    sel_tvt,
    sel_tjac,
    sel_b,
    sel_lift,
    same_v,
    same_tv,
    same_f,
    same_vt,
    keep,
    table_ref,
    motion_ref,
    step_ref,
    own_ref,
    theirs_ref,
    space_ref,
    trace_ref,
    flux_ref,
    lifting_ref,
    state,
    first,
    second,
    ones,
    parts,
    vert_send,
    vert_recv,
    min_t,
    min_s,
    slab_send,
    slab_recv,
    peer_send,
    peer_recv,
    vert_sems,
    min_t_sems,
    min_s_sems,
    slab_sems,
    peer_sems,
):
    num_vars, basis, rows, trace_rows, num_faces, slabs, peers, chunk = sizes
    elems = conserved_ref.shape[2]
    shared = share_ref.shape[1]
    verts = vertex_ref.shape[1]
    slab_width = slab_send.shape[2]
    peer_width = peer_send.shape[2]
    send_rows = slab_send.shape[1]
    s = lax.axis_index("shock")
    t = lax.axis_index("trans")

    barrier = pltpu.get_barrier_semaphore()
    for o in range(1, peers):
        pl.semaphore_signal(
            barrier, inc=1, device_id=(s, lax.rem(t + o, peers)), device_id_type=MESH
        )
    for o in range(1, slabs):
        pl.semaphore_signal(
            barrier, inc=1, device_id=(lax.rem(s + o, slabs), t), device_id_type=MESH
        )

    def spread(velocity):
        high, low = split(velocity)
        rest = velocity - high.astype(F32) - low.astype(F32)
        return high.astype(F32), low.astype(F32), rest

    parts[...] = jnp.zeros_like(parts)
    for i, piece in enumerate(spread(vertex_ref[...])):
        parts[8 * i : 8 * i + 3, :verts] = piece
    share = jnp.concatenate([share_ref[0:1, :], share_ref[1:2, :]], axis=1)
    sent = dot(parts[:, :verts].astype(BF16), ones_at(share, verts))
    sent = sent[0:8] + sent[8:16] + sent[16:24]
    vert_send[0] = sent[:, :shared]
    vert_send[1] = sent[:, shared:]
    pl.semaphore_wait(barrier, peers - 1 + slabs - 1)

    def to_lower(source, dest, sems):
        return pltpu.make_async_remote_copy(
            src_ref=source.at[0],
            dst_ref=dest.at[1],
            send_sem=sems.at[0],
            recv_sem=sems.at[3],
            device_id=(s - 1, t),
            device_id_type=MESH,
        )

    def to_upper(source, dest, sems):
        return pltpu.make_async_remote_copy(
            src_ref=source.at[1],
            dst_ref=dest.at[0],
            send_sem=sems.at[1],
            recv_sem=sems.at[2],
            device_id=(s + 1, t),
            device_id_type=MESH,
        )

    def start_slab(source, dest, sems):
        @pl.when(s > 0)
        def _():
            to_lower(source, dest, sems).start()

        @pl.when(s < slabs - 1)
        def _():
            to_upper(source, dest, sems).start()

    def finish_slab(source, dest, sems):
        @pl.when(s > 0)
        def _():
            to_lower(source, dest, sems).wait_send()
            to_upper(source, dest, sems).wait_recv()

        @pl.when(s < slabs - 1)
        def _():
            to_upper(source, dest, sems).wait_send()
            to_lower(source, dest, sems).wait_recv()

        @pl.when(s == 0)
        def _():
            dest[0] = jnp.zeros(dest.shape[1:], F32)

        @pl.when(s == slabs - 1)
        def _():
            dest[1] = jnp.zeros(dest.shape[1:], F32)

    start_slab(vert_send, vert_recv, vert_sems)

    jac_wide = exact(sel_jac[...], exact(jac_ref[...], sel_vt[...]))
    der_wide = exact(sel_der[...], exact(der_ref[...], sel_bt[...]))
    both = jac_wide * der_wide
    space_ref[0:rows, :] = operator(both[:rows] + both[rows : 2 * rows] + both[2 * rows :])
    for d in range(3):
        space_ref[(d + 1) * rows : (d + 2) * rows, :] = operator(
            der_wide[d * rows : (d + 1) * rows] * same_v[...]
        )
    for v in range(num_vars):
        state[v * basis : (v + 1) * basis, :] = conserved_ref[v]
    state[num_vars * basis :, :] = jnp.zeros((rows - num_vars * basis, elems), F32)

    def counted(columns, low, count):
        places = lax.broadcasted_iota(jnp.int32, (count, chunk), 0) + low
        total = jnp.where(places == corner_ref[0:1, columns], 1.0, 0.0)
        for i in range(1, 4):
            total = total + jnp.where(places == corner_ref[i : i + 1, columns], 1.0, 0.0)
        return total.astype(BF16)

    own_parts = parts[:, :verts].astype(BF16)

    def own_corner(c, carry):
        columns = pl.ds(pl.multiple_of(c * chunk, chunk), chunk)
        found = dot(own_parts, counted(columns, 0, verts))
        motion_ref[:, columns] = found[0:8] + found[8:16] + found[16:24]
        return carry

    lax.fori_loop(0, elems // chunk, own_corner, 0)
    finish_slab(vert_send, vert_recv, vert_sems)
    for side in range(2):
        place = verts + side * shared
        for i, piece in enumerate(spread(vert_recv[side])):
            parts[8 * i : 8 * i + 8, place : place + shared] = piece
    far_parts = parts[:, verts:].astype(BF16)

    def far_corner(c, smallest):
        columns = pl.ds(pl.multiple_of(c * chunk, chunk), chunk)
        found = dot(far_parts, counted(columns, verts, 2 * shared))
        vel = 0.25 * (motion_ref[:, columns] + (found[0:8] + found[8:16] + found[16:24]))
        size = scalars_ref[0:1, columns]
        speed = (
            scalars_ref[1:2, columns] + jnp.abs(vel[0:1]) + jnp.abs(vel[1:2]) + jnp.abs(vel[2:3])
        )
        motion_ref[0:3, columns] = vel[0:3]
        motion_ref[3:4, columns] = 1.0 / size
        motion_ref[4:5, columns] = speed
        return jnp.minimum(smallest, jnp.min(size / speed, axis=1, keepdims=True))

    smallest = lax.fori_loop(0, elems // chunk, far_corner, jnp.full((1, 1), jnp.inf, F32))

    def min_copy(buffer, sems, place, count, o, along_trans):
        to = lax.rem(place + o, count)
        return pltpu.make_async_remote_copy(
            src_ref=buffer.at[place],
            dst_ref=buffer.at[place],
            send_sem=sems.at[0, o],
            recv_sem=sems.at[1, place],
            device_id=(s, to) if along_trans else (to, t),
            device_id_type=MESH,
        )

    def min_wait(buffer, sems, place, count, along_trans):
        for o in range(1, count):
            origin = lax.rem(place + count - o, count)
            pltpu.make_async_remote_copy(
                src_ref=buffer.at[origin],
                dst_ref=buffer.at[origin],
                send_sem=sems.at[0, o],
                recv_sem=sems.at[1, origin],
                device_id=(s, origin) if along_trans else (origin, t),
                device_id_type=MESH,
            ).wait_recv()
            min_copy(buffer, sems, place, count, o, along_trans).wait_send()

    min_t[t] = jnp.broadcast_to(smallest, min_t.shape[1:])
    for o in range(1, peers):
        min_copy(min_t, min_t_sems, t, peers, o, True).start()

    def space_step(source, dest):
        def one(c, carry):
            columns = pl.ds(pl.multiple_of(c * chunk, chunk), chunk)
            dest[:, columns] = apply_space(
                space_ref[...],
                source[:, columns],
                motion_ref[:, columns],
                motion_ref[3:4, columns],
                rows,
            )
            return carry

        lax.fori_loop(0, elems // chunk, one, 0)

    space_step(state, first)
    min_wait(min_t, min_t_sems, t, peers, True)
    best = min_t[0]
    for i in range(1, peers):
        best = jnp.minimum(best, min_t[i])
    min_s[s] = best
    for o in range(1, slabs):
        min_copy(min_s, min_s_sems, s, slabs, o, False).start()
    space_step(first, second)

    res_wide = exact(sel_res[...], exact(res_ref[...], sel_bt[...]))
    for k in range(num_faces):
        trace_ref[k * trace_rows : (k + 1) * trace_rows, :] = operator(
            res_wide[k * trace_rows : (k + 1) * trace_rows] * same_tv[...] + keep[...]
        )
    tjac_wide = exact(sel_tjac[...], exact(jac_ref[...], sel_tvt[...]))
    for d in range(3):
        flux_ref[d * trace_rows : (d + 1) * trace_rows, :] = operator(
            tjac_wide[d * trace_rows : (d + 1) * trace_rows] * same_f[...]
        )
    lift_wide = exact(sel_b[...], exact(lift_ref[...], sel_lift[...]))
    spread_v = jnp.concatenate([same_vt[...]] * num_faces, axis=1)
    lifting_ref[...] = operator(lift_wide * spread_v)
    ones[...] = ones_at(bound_index_ref[0:1, :], elems)

    min_wait(min_s, min_s_sems, s, slabs, False)
    best = min_s[0]
    for i in range(1, slabs):
        best = jnp.minimum(best, min_s[i])
    step = CFL_NUMBER * best
    step_ref[...] = step
    dt = step[0:1, 0:1]
    table_ref[...] = (
        state[...] - (0.5 * dt) * first[...] + (dt * dt * (1.0 / 6.0)) * second[...]
    )
    flat = num_vars * basis
    table_ref[flat : flat + 1, :] = motion_ref[4:5, :]
    high, low = split(table_ref[...])
    trace = gather_trace(
        jnp.concatenate([high, low], axis=0),
        ones[...],
        bound_index_ref[1:2, :],
        trace_ref[...],
        rows,
        trace_rows,
        num_faces,
    )
    own_ref[...] = trace
    cut = trace[:send_rows]
    slab_send[0] = cut[:, :slab_width]
    slab_send[1] = cut[:, slab_width : 2 * slab_width]
    for q in range(peers):
        low_end = 2 * slab_width + q * peer_width
        peer_send[q] = cut[:, low_end : low_end + peer_width]
    start_slab(slab_send, slab_recv, slab_sems)

    def peer_copy(o):
        to = lax.rem(t + o, peers)
        return pltpu.make_async_remote_copy(
            src_ref=peer_send.at[to],
            dst_ref=peer_recv.at[t],
            send_sem=peer_sems.at[0, o],
            recv_sem=peer_sems.at[1, t],
            device_id=(s, to),
            device_id_type=MESH,
        )

    for o in range(1, peers):
        peer_copy(o).start()
    peer_recv[t] = jnp.zeros(peer_recv.shape[1:], F32)
    theirs_ref[...] = jnp.zeros_like(theirs_ref)
    for o in range(1, peers):
        peer_copy(o).wait_send()
        origin = lax.rem(t + peers - o, peers)
        pltpu.make_async_remote_copy(
            src_ref=peer_send.at[origin],
            dst_ref=peer_recv.at[origin],
            send_sem=peer_sems.at[0, o],
            recv_sem=peer_sems.at[1, origin],
            device_id=(s, origin),
            device_id_type=MESH,
        ).wait_recv()
    for q in range(peers):
        low_end = 2 * slab_width + q * peer_width
        theirs_ref[:send_rows, low_end : low_end + peer_width] = peer_recv[q]
    finish_slab(slab_send, slab_recv, slab_sems)
    for side in range(2):
        theirs_ref[:send_rows, side * slab_width : (side + 1) * slab_width] = slab_recv[side]


def back_kernel(
    sizes,
    table_ref,
    motion_ref,
    own_ref,
    theirs_ref,
    space_ref,
    trace_ref,
    flux_ref,
    lifting_ref,
    bound_index_ref,
    bound_values_ref,
    inner_elem_ref,
    inner_face_ref,
    inner_normal_ref,
    rate_ref,
    table,
    ones,
    ones_bound,
    total,
):
    num_vars, basis, rows, trace_rows, num_faces, flat_trace, chunk, tile = sizes
    elems = table_ref.shape[1]
    high, low = split(table_ref[...])
    table[:rows, :] = high
    table[rows:, :] = low

    def normal_flux(jump, normal):
        product = dot(flux_ref[...], operand(jump))
        result = normal[0:1] * product[:trace_rows]
        for d in range(1, 3):
            result = result + normal[d : d + 1] * product[d * trace_rows : (d + 1) * trace_rows]
        return result

    def lifted(flux, faces, where_ones):
        high = flux.astype(BF16).astype(F32)
        low = flux - high
        highs = [jnp.where(faces == k, high, 0.0).astype(BF16) for k in range(num_faces)]
        lows = [jnp.where(faces == k, low, 0.0).astype(BF16) for k in range(num_faces)]
        value = dot(lifting_ref[...], jnp.concatenate(highs + lows + highs, axis=0))
        pair = jnp.concatenate(split(value), axis=0)
        return lax.dot_general(
            pair, where_ones, (((1,), (1,)), ((), ())), preferred_element_type=F32
        )

    faces = bound_index_ref[1:2, :]
    ones_bound[...] = ones_at(bound_index_ref[0:1, :], elems)
    own, theirs = own_ref[...], theirs_ref[...]
    jump = theirs - own
    bound = jnp.maximum(
        own[flat_trace : flat_trace + 1, :], theirs[flat_trace : flat_trace + 1, :]
    )
    flux = normal_flux(jump, bound_values_ref[...]) - bound * jump
    total[...] = lifted((0.5 * bound_values_ref[3:4, :]) * flux, faces, ones_bound[...])

    def inner(j, carry):
        columns = pl.ds(pl.multiple_of(j * tile, tile), tile)
        index = jnp.concatenate(
            [inner_elem_ref[0:1, columns], inner_elem_ref[1:2, columns]], axis=1
        )
        face = jnp.concatenate(
            [inner_face_ref[0:1, columns], inner_face_ref[1:2, columns]], axis=1
        )
        ones[...] = ones_at(index, elems)
        trace = gather_trace(
            table[...], ones[...], face, trace_ref[...], rows, trace_rows, num_faces
        )
        jump = trace[:, tile:] - trace[:, :tile]
        bound = jnp.maximum(
            trace[flat_trace : flat_trace + 1, :tile], trace[flat_trace : flat_trace + 1, tile:]
        )
        flow = normal_flux(jump, inner_normal_ref[:, columns])
        drop = bound * jump
        flux = 0.5 * jnp.concatenate([flow - drop, flow + drop], axis=1)
        total[...] += lifted(flux, face, ones[...])
        return carry

    lax.fori_loop(0, inner_elem_ref.shape[1] // tile, inner, 0)

    def finish(c, carry):
        columns = pl.ds(pl.multiple_of(c * chunk, chunk), chunk)
        inverse = motion_ref[3:4, columns]
        value = apply_space(
            space_ref[...], table_ref[:, columns], motion_ref[:, columns], inverse, rows
        )
        face_term = total[:rows, columns] + total[rows:, columns]
        rate = -(value + face_term * inverse)
        for v in range(num_vars):
            rate_ref[v, :, columns] = rate[v * basis : (v + 1) * basis]
        return carry

    lax.fori_loop(0, elems // chunk, finish, 0)


def body(
    conserved,
    cell_size,
    sound_speed,
    jacobian,
    derivative,
    restriction,
    lifting,
    vertex_velocity,
    share_index,
    elem_vertex,
    inner_elem,
    inner_face,
    inner_normal,
    slab_elem,
    slab_face,
    slab_normal,
    peer_elem,
    peer_face,
    peer_normal,
    peer_count,
):
    num_vars, basis, elems = conserved.shape
    num_faces, face_basis = restriction.shape[:2]
    slabs, peers = lax.axis_size("shock"), lax.axis_size("trans")
    slab_width, peer_width = slab_elem.shape[1], peer_elem.shape[1]
    verts, shared = vertex_velocity.shape[1], share_index.shape[1]
    rows = up_to(num_vars * basis + 1, 16)
    flat_trace = num_vars * face_basis
    trace_rows = up_to(flat_trace + 1, 16)
    send_rows = up_to(flat_trace + 1, 8)
    sides = 2 * slab_width + peers * peer_width
    chunk = min(512, elems)
    tile = min(512, inner_elem.shape[1])

    bound_index = jnp.stack(
        [
            jnp.concatenate([slab_elem.reshape(-1), peer_elem.reshape(-1)]),
            jnp.concatenate([slab_face.reshape(-1), peer_face.reshape(-1)]),
        ]
    )
    live = (jnp.arange(peer_width)[None, :] < peer_count).astype(F32).reshape(1, -1)
    bound_values = jnp.concatenate(
        [
            jnp.concatenate([slab_normal.reshape(3, -1), peer_normal.reshape(3, -1)], axis=1),
            jnp.concatenate([jnp.ones((1, 2 * slab_width), F32), live], axis=1),
        ],
        axis=0,
    )
    spreads = [
        jnp.asarray(a)
        for a in selections(num_vars, basis, face_basis, num_faces, rows, trace_rows)
    ]
    vmem = pl.BlockSpec(memory_space=pltpu.VMEM)
    out_shapes = (
        jax.ShapeDtypeStruct((rows, elems), F32),
        jax.ShapeDtypeStruct((8, elems), F32),
        jax.ShapeDtypeStruct((8, 128), F32),
        jax.ShapeDtypeStruct((trace_rows, sides), F32),
        jax.ShapeDtypeStruct((trace_rows, sides), F32),
        jax.ShapeDtypeStruct((4 * rows, 3 * rows), BF16),
        jax.ShapeDtypeStruct((num_faces * trace_rows, 3 * rows), BF16),
        jax.ShapeDtypeStruct((3 * trace_rows, 3 * trace_rows), BF16),
        jax.ShapeDtypeStruct((rows, 3 * num_faces * trace_rows), BF16),
    )
    front_args = [
        conserved,
        jnp.stack([cell_size, sound_speed]),
        vertex_velocity,
        share_index,
        elem_vertex,
        jacobian.reshape(3 * num_vars, num_vars),
        derivative.reshape(3 * basis, basis),
        restriction.reshape(num_faces * face_basis, basis),
        jnp.transpose(lifting, (1, 0, 2)).reshape(basis, num_faces * face_basis),
        bound_index,
        *spreads,
    ]
    dma = pltpu.SemaphoreType.DMA
    table, motion, step, own, theirs, space, trace, flux, lift = pl.pallas_call(
        functools.partial(
            front_kernel,
            (num_vars, basis, rows, trace_rows, num_faces, slabs, peers, chunk),
        ),
        out_shape=out_shapes,
        in_specs=[vmem] * len(front_args),
        out_specs=[vmem] * len(out_shapes),
        scratch_shapes=[
            pltpu.VMEM((rows, elems), F32),
            pltpu.VMEM((rows, elems), F32),
            pltpu.VMEM((rows, elems), F32),
            pltpu.VMEM((elems, sides), BF16),
            pltpu.VMEM((24, verts + 2 * shared), F32),
            pltpu.VMEM((2, 8, shared), F32),
            pltpu.VMEM((2, 8, shared), F32),
            pltpu.VMEM((peers, 8, 128), F32),
            pltpu.VMEM((slabs, 8, 128), F32),
            pltpu.VMEM((2, send_rows, slab_width), F32),
            pltpu.VMEM((2, send_rows, slab_width), F32),
            pltpu.VMEM((peers, send_rows, peer_width), F32),
            pltpu.VMEM((peers, send_rows, peer_width), F32),
            dma((4,)),
            dma((2, peers)),
            dma((2, slabs)),
            dma((4,)),
            dma((2, peers)),
        ],
        compiler_params=pltpu.CompilerParams(
            collective_id=0, has_side_effects=True, vmem_limit_bytes=VMEM_BYTES
        ),
        name="front",
    )(*front_args)

    back_args = [
        table,
        motion,
        own,
        theirs,
        space,
        trace,
        flux,
        lift,
        bound_index,
        bound_values,
        inner_elem,
        inner_face,
        inner_normal,
    ]
    rate = pl.pallas_call(
        functools.partial(
            back_kernel,
            (num_vars, basis, rows, trace_rows, num_faces, flat_trace, chunk, tile),
        ),
        out_shape=jax.ShapeDtypeStruct((num_vars, basis, elems), F32),
        in_specs=[vmem] * len(back_args),
        out_specs=vmem,
        scratch_shapes=[
            pltpu.VMEM((2 * rows, elems), BF16),
            pltpu.VMEM((elems, 2 * tile), BF16),
            pltpu.VMEM((elems, sides), BF16),
            pltpu.VMEM((2 * rows, elems), F32),
        ],
        compiler_params=pltpu.CompilerParams(vmem_limit_bytes=VMEM_BYTES),
        name="back",
    )(*back_args)
    return rate, step[0, 0]


def solution(mesh):
    both = ("shock", "trans")
    last2, last3 = P(None, both), P(None, None, both)
    return jax.shard_map(
        body,
        mesh=mesh,
        in_specs=(
            last3,
            P(both),
            P(both),
            P(),
            P(),
            P(),
            P(),
            last2,
            last2,
            last2,
            last2,
            last2,
            last2,
            last2,
            last2,
            last3,
            last2,
            last2,
            last3,
            last2,
        ),
        out_specs=(last3, P()),
        check_vma=False,
    )
```

profile of v0, /device:TPU:0, one launch (start us, length us, event | category | flops | bytes accessed | tf_op | source)
XLA Modules:
  0.0 80.0 jit_solution(6058142158967881948)
XLA Ops:
  0.6 0.0 copy-start
  0.6 0.7 copy.57
  1.3 0.8 reshape.67
  2.1 0.0 copy-start.1
  2.1 0.7 copy.58
  2.8 0.8 reshape.69
  3.6 0.6 pad_add_fusion.bound_index_ref
  4.2 0.0 copy-start.2
  4.2 0.0 copy-start.3
  4.2 0.0 copy-start.4
  4.2 0.0 copy-start.5
  4.2 3.0 %copy.46.conserved_ref = f32[11,10,2048]{2,1,0:T(8,128)} copy(f32[11,10,2048]{2,0,1:T(8,128)} %param.34) | data formatting | bytes 1802240 | tf_op args[0]
  7.2 0.0 copy-done
  7.2 0.0 copy-start.6
  7.3 0.0 copy-start.8
  7.3 0.0 copy-start.7
  7.3 0.6 reshape.72.jac_ref
  7.9 0.0 copy-done.1
  7.9 0.6 reshape.73.der_ref
  8.5 0.0 copy-done.2
  8.5 0.6 reshape.64.res_ref
  9.1 0.0 copy-done.3
  9.1 0.1 copy.53
  9.2 0.7 reshape.74.lift_ref
  9.9 0.0 copy-done.4
  9.9 0.0 copy-done.5
  9.9 0.6 pad_maximum_fusion.scalars_ref
  10.5 26.4 %front.1 = (f32[112,2048]{1,0:T(8,128)}, f32[8,2048]{1,0:T(8,128)}, f32[8,128]{1,0:T(8,128)}, f32[80,768]{1,0:T(8,128)}, f32[80,768]{1,0:T(8,128)}, /*index=5*/b...) custom-call(f32[11,10,2048]{2,1,0:T(8,128)} %copy.46.conserved_ref, ...), custom_call_target="tpu_custom_call" | custom-call | tf_op jit(solution)/shard_map/front/pallas_call | solution.py:601
  37.0 0.0 copy-done.6
  37.0 0.0 copy-done.8
  37.0 0.1 iota_compare_fusion
  37.1 0.1 convert_element_type.11
  37.2 0.0 copy-done.7
  37.2 0.1 reshape.71
  37.3 0.6 pad_maximum_fusion.1.bound_values_ref
  37.9 38.0 %back.1 = f32[11,10,2048]{2,1,0:T(8,128)} custom-call(f32[112,2048]{1,0:T(8,128)} %get-tuple-element.11.table_ref, f32[8,2048]{1,0:T(8,128)} %get-tuple-element.12.motion_ref, f32[80,768]{1,0:T(8,128)} %get-tuple-element.13.own_ref, f32[80,768]{1,0:T(8,128)} %get-tuple-element.14.theirs_ref, bf16[448,336]{1,0:T(8,128)(2,1)} %get-tuple-element.15.space_ref, ...), custom_call_target="tpu_custom_call" | custom-call | tf_op jit(solution)/shard_map/back/pallas_call | solution.py:650
  75.8 2.9 %copy.50 = f32[11,10,2048]{2,0,1:T(8,128)} copy(f32[11,10,2048]{2,1,0:T(8,128)} %back.1) | data formatting | bytes 1802240
  78.8 1.2 %slice.3 = f32[1,1]{1,0:T(1,128)} slice(f32[8,128]{1,0:T(8,128)} %get-tuple-element.19), slice={[0:1], [0:1]} | slice | bytes 8 | tf_op jit(solution)/shard_map/slice | solution.py:667
  (9 shorter events, 0.1 us)
Async XLA Ops:
  0.6 6.6 %copy-start = (f32[3,11,11]{2,0,1:T(4,128)S(1)}, f32[3,11,11]{2,0,1:T(4,128)}, u32[]{:S(2)}) copy-start(f32[3,11,11]{2,0,1:T(4,128)} %param.37) | copy-start | bytes 4360
  2.1 5.8 %copy-start.1 = (f32[3,10,10]{2,0,1:T(4,128)S(1)}, f32[3,10,10]{2,0,1:T(4,128)}, u32[]{:S(2)}) copy-start(f32[3,10,10]{2,0,1:T(4,128)} %param.38) | copy-start | bytes 3604
  4.2 4.3 %copy-start.2 = (f32[4,6,10]{2,0,1:T(4,128)S(1)}, f32[4,6,10]{2,0,1:T(4,128)}, u32[]{:S(2)}) copy-start(f32[4,6,10]{2,0,1:T(4,128)} %param.39) | copy-start | bytes 2884
  4.2 4.9 %copy-start.3 = (f32[4,10,6]{1,0,2:T(4,128)S(1)}, f32[4,10,6]{1,0,2:T(4,128)}, u32[]{:S(2)}) copy-start(f32[4,10,6]{1,0,2:T(4,128)} %param.40) | copy-start | bytes 2884
  4.2 5.7 %copy-start.4 = (f32[2048]{0:T(1024)S(1)}, f32[2048]{0:T(1024)}, u32[]{:S(2)}) copy-start(f32[2048]{0:T(1024)} %param.36) | copy-start | bytes 24580
  4.2 5.7 %copy-start.5 = (f32[2048]{0:T(1024)S(1)}, f32[2048]{0:T(1024)}, u32[]{:S(2)}) copy-start(f32[2048]{0:T(1024)} %param.35) | copy-start | bytes 24580
  7.2 29.7 %copy-start.6 = (f32[3,2,256]{2,1,0:T(2,128)S(1)}, f32[3,2,256]{2,1,0:T(2,128)}, u32[]{:S(2)}) copy-start(f32[3,2,256]{2,1,0:T(2,128)} %param.49) | copy-start | bytes 18436
  7.3 29.7 %copy-start.8 = (s32[4,1]{0,1:T(1,128)S(1)}, s32[4,1]{0,1:T(1,128)}, u32[]{:S(2)}) copy-start(s32[4,1]{0,1:T(1,128)} %param.53) | copy-start | bytes 52
  7.3 29.9 %copy-start.7 = (f32[3,4,64]{2,1,0:T(4,128)S(1)}, f32[3,4,64]{2,1,0:T(4,128)}, u32[]{:S(2)}) copy-start(f32[3,4,64]{2,1,0:T(4,128)} %param.52) | copy-start | bytes 9220
where the time goes:
time: 80.4 us; the launch traced here: 80 us
  Pallas kernels  64.4 us (80%)
  local copies, waits for them, and re-layouts  12.9 us (16%)
  other arithmetic  1.94 us (2%)
    pallas_call x1, Pallas kernels, body(): pl.pallas_call(functools.partial(back_kernel, (num_vars, basis, rows, tra...  38 us
    pallas_call x1, Pallas kernels, body(): pl.pallas_call(functools.partial(front_kernel, (num_vars, basis, rows, tr...  26.4 us
    unnamed x24, local copies, waits for them, and re-layouts  7.42 us

commit v1 on v0

--- a/solution.py
+++ b/solution.py
@@ -19,10 +19,16 @@
     return -(-value // multiple) * multiple
 
 
-def selections(num_vars, basis, face_basis, faces, rows, trace_rows):
+def selections(num_vars, basis, face_basis, faces, rows, lift_rows, trace_rows):
     flat, flat_t = num_vars * basis, num_vars * face_basis
     row, trow = np.arange(rows), np.arange(trace_rows)
-    row_v, row_b = np.where(row < flat, row // basis, -1), np.where(row < flat, row % basis, -1)
+    row_v, row_b = (
+        np.where(row < flat, row % num_vars, -1),
+        np.where(row < flat, row // num_vars, -1),
+    )
+    lift_v, lift_b = (
+        np.pad(a, (0, lift_rows - rows), constant_values=-1) for a in (row_v, row_b)
+    )
     trow_v = np.where(trow < flat_t, trow // face_basis, -2)
     trow_f = np.where(trow < flat_t, trow % face_basis, -2)
 
@@ -32,10 +38,11 @@
     def block(target, count, copies):
         out = np.zeros((copies, target.size, copies * count), np.float32)
         for k in range(copies):
-            out[k, :, k * count : (k + 1) * count] = pick(target, count)
+            out[k, :, k::copies] = pick(target, count)
         return out.reshape(copies * target.size, copies * count)
 
     same_v = (row_v[:, None] == row_v[None, :]) & (row_v[:, None] >= 0)
+    same_vt = (lift_v[:, None] == trow_v[None, :]) & (lift_v[:, None] >= 0)
     same_tv = (trow_v[:, None] == row_v[None, :]) & (trow_v[:, None] >= 0)
     same_f = (trow_f[:, None] == trow_f[None, :]) & (trow_f[:, None] >= 0)
     keep = np.zeros((trace_rows, rows), np.float32)
@@ -48,12 +55,12 @@
         block(trow_f, face_basis, faces),
         np.ascontiguousarray(pick(trow_v, num_vars).T),
         block(trow_v, num_vars, 3),
-        pick(row_b, basis),
+        pick(lift_b, basis),
         np.ascontiguousarray(block(trow_f, face_basis, faces).T),
         same_v.astype(np.float32),
         same_tv.astype(np.float32),
         same_f.astype(np.float32),
-        np.ascontiguousarray(same_tv.T.astype(np.float32)),
+        same_vt.astype(np.float32),
         keep,
     ]
 
@@ -107,7 +114,8 @@
 def front_kernel(
     sizes,
     conserved_ref,
-    scalars_ref,
+    size_ref,
+    sound_ref,
     vertex_ref,
     share_ref,
     corner_ref,
@@ -115,7 +123,13 @@
     der_ref,
     res_ref,
     lift_ref,
-    bound_index_ref,
+    slab_elem_ref,
+    slab_face_ref,
+    peer_elem_ref,
+    peer_face_ref,
+    slab_normal_ref,
+    peer_normal_ref,
+    count_ref,
     sel_vt,
     sel_bt,
     sel_jac,
@@ -139,11 +153,17 @@
     trace_ref,
     flux_ref,
     lifting_ref,
+    bound_index_ref,
+    bound_values_ref,
     state,
     first,
     second,
     ones,
     parts,
+    jac,
+    der,
+    res,
+    lift,
     vert_send,
     vert_recv,
     min_t,
@@ -243,16 +263,20 @@
 
     start_slab(vert_send, vert_recv, vert_sems)
 
-    jac_wide = exact(sel_jac[...], exact(jac_ref[...], sel_vt[...]))
-    der_wide = exact(sel_der[...], exact(der_ref[...], sel_bt[...]))
+    for small, held in ((jac_ref, jac), (der_ref, der), (res_ref, res), (lift_ref, lift)):
+        count = small.shape[1]
+        for i in range(small.shape[0]):
+            held[i * count : (i + 1) * count, :] = small[i]
+    jac_wide = exact(sel_jac[...], exact(jac[...], sel_vt[...]))
+    der_wide = exact(sel_der[...], exact(der[...], sel_bt[...]))
     both = jac_wide * der_wide
     space_ref[0:rows, :] = operator(both[:rows] + both[rows : 2 * rows] + both[2 * rows :])
     for d in range(3):
         space_ref[(d + 1) * rows : (d + 2) * rows, :] = operator(
             der_wide[d * rows : (d + 1) * rows] * same_v[...]
         )
-    for v in range(num_vars):
-        state[v * basis : (v + 1) * basis, :] = conserved_ref[v]
+    for b in range(basis):
+        state[b * num_vars : (b + 1) * num_vars, :] = conserved_ref[b]
     state[num_vars * basis :, :] = jnp.zeros((rows - num_vars * basis, elems), F32)
 
     def counted(columns, low, count):
@@ -282,9 +306,9 @@
         columns = pl.ds(pl.multiple_of(c * chunk, chunk), chunk)
         found = dot(far_parts, counted(columns, verts, 2 * shared))
         vel = 0.25 * (motion_ref[:, columns] + (found[0:8] + found[8:16] + found[16:24]))
-        size = scalars_ref[0:1, columns]
+        size = size_ref[0:1, columns]
         speed = (
-            scalars_ref[1:2, columns] + jnp.abs(vel[0:1]) + jnp.abs(vel[1:2]) + jnp.abs(vel[2:3])
+            sound_ref[0:1, columns] + jnp.abs(vel[0:1]) + jnp.abs(vel[1:2]) + jnp.abs(vel[2:3])
         )
         motion_ref[0:3, columns] = vel[0:3]
         motion_ref[3:4, columns] = 1.0 / size
@@ -345,19 +369,56 @@
         min_copy(min_s, min_s_sems, s, slabs, o, False).start()
     space_step(first, second)
 
-    res_wide = exact(sel_res[...], exact(res_ref[...], sel_bt[...]))
+    res_wide = exact(sel_res[...], exact(res[...], sel_bt[...]))
     for k in range(num_faces):
         trace_ref[k * trace_rows : (k + 1) * trace_rows, :] = operator(
             res_wide[k * trace_rows : (k + 1) * trace_rows] * same_tv[...] + keep[...]
         )
-    tjac_wide = exact(sel_tjac[...], exact(jac_ref[...], sel_tvt[...]))
+    tjac_wide = exact(sel_tjac[...], exact(jac[...], sel_tvt[...]))
     for d in range(3):
         flux_ref[d * trace_rows : (d + 1) * trace_rows, :] = operator(
             tjac_wide[d * trace_rows : (d + 1) * trace_rows] * same_f[...]
         )
-    lift_wide = exact(sel_b[...], exact(lift_ref[...], sel_lift[...]))
+    lift_rows = lax.dot_general(
+        sel_b[...],
+        lift[...],
+        (((1,), (1,)), ((), ())),
+        precision=lax.Precision.HIGHEST,
+        preferred_element_type=F32,
+    )
+    lift_wide = exact(lift_rows, sel_lift[...])
     spread_v = jnp.concatenate([same_vt[...]] * num_faces, axis=1)
     lifting_ref[...] = operator(lift_wide * spread_v)
+    for row, slab_ref, peer_ref in (
+        (0, slab_elem_ref, peer_elem_ref),
+        (1, slab_face_ref, peer_face_ref),
+    ):
+        for side in range(2):
+            bound_index_ref[row : row + 1, side * slab_width : (side + 1) * slab_width] = slab_ref[
+                side : side + 1, :
+            ]
+        for q in range(peers):
+            low_end = 2 * slab_width + q * peer_width
+            bound_index_ref[row : row + 1, low_end : low_end + peer_width] = peer_ref[
+                q : q + 1, :
+            ]
+    for d in range(3):
+        for side in range(2):
+            bound_values_ref[d : d + 1, side * slab_width : (side + 1) * slab_width] = (
+                slab_normal_ref[d, side : side + 1, :]
+            )
+        for q in range(peers):
+            low_end = 2 * slab_width + q * peer_width
+            bound_values_ref[d : d + 1, low_end : low_end + peer_width] = peer_normal_ref[
+                d, q : q + 1, :
+            ]
+    bound_values_ref[3:4, : 2 * slab_width] = jnp.ones((1, 2 * slab_width), F32)
+    slot = lax.broadcasted_iota(jnp.int32, (1, peer_width), 1)
+    for q in range(peers):
+        low_end = 2 * slab_width + q * peer_width
+        bound_values_ref[3:4, low_end : low_end + peer_width] = jnp.where(
+            slot < count_ref[0:1, q : q + 1], 1.0, 0.0
+        )
     ones[...] = ones_at(bound_index_ref[0:1, :], elems)
 
     min_wait(min_s, min_s_sems, s, slabs, False)
@@ -440,7 +501,9 @@
     inner_elem_ref,
     inner_face_ref,
     inner_normal_ref,
+    step_ref,
     rate_ref,
+    step_out_ref,
     table,
     ones,
     ones_bound,
@@ -448,6 +511,8 @@
 ):
     num_vars, basis, rows, trace_rows, num_faces, flat_trace, chunk, tile = sizes
     elems = table_ref.shape[1]
+    lift_rows = lifting_ref.shape[0]
+    step_out_ref[0, 0] = step_ref[0, 0]
     high, low = split(table_ref[...])
     table[:rows, :] = high
     table[rows:, :] = low
@@ -467,7 +532,7 @@
         value = dot(lifting_ref[...], jnp.concatenate(highs + lows + highs, axis=0))
         pair = jnp.concatenate(split(value), axis=0)
         return lax.dot_general(
-            pair, where_ones, (((1,), (1,)), ((), ())), preferred_element_type=F32
+            where_ones, pair, (((1,), (1,)), ((), ())), preferred_element_type=F32
         )
 
     faces = bound_index_ref[1:2, :]
@@ -510,10 +575,10 @@
         value = apply_space(
             space_ref[...], table_ref[:, columns], motion_ref[:, columns], inverse, rows
         )
-        face_term = total[:rows, columns] + total[rows:, columns]
-        rate = -(value + face_term * inverse)
-        for v in range(num_vars):
-            rate_ref[v, :, columns] = rate[v * basis : (v + 1) * basis]
+        face_term = jnp.transpose(total[columns, :lift_rows] + total[columns, lift_rows:])
+        rate = -(value + face_term[:rows] * inverse)
+        for b in range(basis):
+            rate_ref[b, :, columns] = rate[b * num_vars : (b + 1) * num_vars]
         return carry
 
     lax.fori_loop(0, elems // chunk, finish, 0)
@@ -547,6 +612,7 @@
     slab_width, peer_width = slab_elem.shape[1], peer_elem.shape[1]
     verts, shared = vertex_velocity.shape[1], share_index.shape[1]
     rows = up_to(num_vars * basis + 1, 16)
+    lift_rows = up_to(rows, 128)
     flat_trace = num_vars * face_basis
     trace_rows = up_to(flat_trace + 1, 16)
     send_rows = up_to(flat_trace + 1, 8)
@@ -554,23 +620,9 @@
     chunk = min(512, elems)
     tile = min(512, inner_elem.shape[1])
 
-    bound_index = jnp.stack(
-        [
-            jnp.concatenate([slab_elem.reshape(-1), peer_elem.reshape(-1)]),
-            jnp.concatenate([slab_face.reshape(-1), peer_face.reshape(-1)]),
-        ]
-    )
-    live = (jnp.arange(peer_width)[None, :] < peer_count).astype(F32).reshape(1, -1)
-    bound_values = jnp.concatenate(
-        [
-            jnp.concatenate([slab_normal.reshape(3, -1), peer_normal.reshape(3, -1)], axis=1),
-            jnp.concatenate([jnp.ones((1, 2 * slab_width), F32), live], axis=1),
-        ],
-        axis=0,
-    )
     spreads = [
         jnp.asarray(a)
-        for a in selections(num_vars, basis, face_basis, num_faces, rows, trace_rows)
+        for a in selections(num_vars, basis, face_basis, num_faces, rows, lift_rows, trace_rows)
     ]
     vmem = pl.BlockSpec(memory_space=pltpu.VMEM)
     out_shapes = (
@@ -582,23 +634,32 @@
         jax.ShapeDtypeStruct((4 * rows, 3 * rows), BF16),
         jax.ShapeDtypeStruct((num_faces * trace_rows, 3 * rows), BF16),
         jax.ShapeDtypeStruct((3 * trace_rows, 3 * trace_rows), BF16),
-        jax.ShapeDtypeStruct((rows, 3 * num_faces * trace_rows), BF16),
+        jax.ShapeDtypeStruct((lift_rows, 3 * num_faces * trace_rows), BF16),
+        jax.ShapeDtypeStruct((2, sides), jnp.int32),
+        jax.ShapeDtypeStruct((4, sides), F32),
     )
     front_args = [
-        conserved,
-        jnp.stack([cell_size, sound_speed]),
+        jnp.transpose(conserved, (1, 0, 2)),
+        cell_size.reshape(1, elems),
+        sound_speed.reshape(1, elems),
         vertex_velocity,
         share_index,
         elem_vertex,
-        jacobian.reshape(3 * num_vars, num_vars),
-        derivative.reshape(3 * basis, basis),
-        restriction.reshape(num_faces * face_basis, basis),
-        jnp.transpose(lifting, (1, 0, 2)).reshape(basis, num_faces * face_basis),
-        bound_index,
+        jnp.transpose(jacobian, (1, 0, 2)),
+        jnp.transpose(derivative, (1, 0, 2)),
+        jnp.transpose(restriction, (1, 0, 2)),
+        jnp.transpose(lifting, (2, 0, 1)),
+        slab_elem,
+        slab_face,
+        peer_elem,
+        peer_face,
+        slab_normal,
+        peer_normal,
+        jnp.transpose(peer_count),
         *spreads,
     ]
     dma = pltpu.SemaphoreType.DMA
-    table, motion, step, own, theirs, space, trace, flux, lift = pl.pallas_call(
+    table, motion, step, own, theirs, space, trace, flux, lift, bound_index, bound_values = pl.pallas_call(
         functools.partial(
             front_kernel,
             (num_vars, basis, rows, trace_rows, num_faces, slabs, peers, chunk),
@@ -612,6 +673,10 @@
             pltpu.VMEM((rows, elems), F32),
             pltpu.VMEM((elems, sides), BF16),
             pltpu.VMEM((24, verts + 2 * shared), F32),
+            pltpu.VMEM((3 * num_vars, num_vars), F32),
+            pltpu.VMEM((3 * basis, basis), F32),
+            pltpu.VMEM((num_faces * face_basis, basis), F32),
+            pltpu.VMEM((num_faces * face_basis, basis), F32),
             pltpu.VMEM((2, 8, shared), F32),
             pltpu.VMEM((2, 8, shared), F32),
             pltpu.VMEM((peers, 8, 128), F32),
@@ -646,25 +711,29 @@
         inner_elem,
         inner_face,
         inner_normal,
+        step,
     ]
-    rate = pl.pallas_call(
+    rate, step = pl.pallas_call(
         functools.partial(
             back_kernel,
             (num_vars, basis, rows, trace_rows, num_faces, flat_trace, chunk, tile),
         ),
-        out_shape=jax.ShapeDtypeStruct((num_vars, basis, elems), F32),
-        in_specs=[vmem] * len(back_args),
-        out_specs=vmem,
+        out_shape=(
+            jax.ShapeDtypeStruct((basis, num_vars, elems), F32),
+            jax.ShapeDtypeStruct((1, 1), F32),
+        ),
+        in_specs=[vmem] * (len(back_args) - 1) + [pl.BlockSpec(memory_space=pltpu.SMEM)],
+        out_specs=(vmem, pl.BlockSpec(memory_space=pltpu.SMEM)),
         scratch_shapes=[
             pltpu.VMEM((2 * rows, elems), BF16),
             pltpu.VMEM((elems, 2 * tile), BF16),
             pltpu.VMEM((elems, sides), BF16),
-            pltpu.VMEM((2 * rows, elems), F32),
+            pltpu.VMEM((elems, 2 * lift_rows), F32),
         ],
         compiler_params=pltpu.CompilerParams(vmem_limit_bytes=VMEM_BYTES),
         name="back",
     )(*back_args)
-    return rate, step[0, 0]
+    return jnp.transpose(rate, (1, 0, 2)), step.reshape(())
 
 
 def solution(mesh):

time: 80.4 us -> 65.4 us (0.81)
  local copies, waits for them, and re-layouts: 12.9 us -> 0 us
  other arithmetic: 1.94 us -> 0 us
    unnamed x24 -> x0, local copies, waits for them, and re-layouts: 7.42 us -> none
    reshape x10 -> x0, local copies, waits for them, and re-layouts: 4.21 us -> none  [the longest x2 0.79 us: body(): jnp.transpose(lifting, (1, 0, 2)).reshape(basis, num_faces * face_basis)]
    another operation x2 -> x0, other arithmetic: 1.23 us -> none  [the longest x1 0.62 us: body(): jnp.stack([cell_size, sound_speed])]
    slice x1 -> x0, local copies, waits for them, and re-layouts: 1.19 us -> none  [body(): return (rate, step[0, 0])]
where the time goes in v1:
time: 65.4 us; the launch traced here: 65.3 us
  Pallas kernels  64.6 us (99%)
    pallas_call x1, Pallas kernels, body(): pl.pallas_call(functools.partial(back_kernel, (num_vars, basis, rows, tra...  37.9 us
    pallas_call x1, Pallas kernels, body(): pl.pallas_call(functools.partial(front_kernel, (num_vars, basis, rows, tr...  26.7 us

profile of v1, /device:TPU:0, one launch (start us, length us, event | category | flops | bytes accessed | tf_op | source)
XLA Modules:
  0.0 65.3 jit_solution(7942886320700596374)
XLA Ops:
  0.6 26.7 %front.1 = (f32[112,2048]{1,0:T(8,128)}, f32[8,2048]{1,0:T(8,128)}, f32[8,128]{1,0:T(8,128)}, f32[80,768]{1,0:T(8,128)}, f32[80,768]{1,0:T(8,128)}, /*index=5*/b...) custom-call(f32[10,11,2048]{2,1,0:T(8,128)} %bitcast.10, ...), custom_call_target="tpu_custom_call" | custom-call | tf_op jit(solution)/shard_map/front/pallas_call | solution.py:662
  27.3 37.9 %back.1 = (f32[10,11,2048]{2,1,0:T(8,128)}, f32[1,1]{1,0:T(1,128)}) custom-call(f32[112,2048]{1,0:T(8,128)} %get-tuple-element.15.table_ref, f32[8,2048]{1,0:T(8,128)} %get-tuple-element.16.motion_ref, f32[80,768]{1,0:T(8,128)} %get-tuple-element.17.own_ref, f32[80,768]{1,0:T(8,128)} %get-tuple-element.18.theirs_ref, ...), custom_call_target="tpu_custom_call" | custom-call | tf_op jit(solution)/shard_map/back/pallas_call | solution.py:716

commit v2 on v1

--- a/solution.py
+++ b/solution.py
@@ -89,8 +89,8 @@
 
 
 def ones_at(index, count):
-    places = lax.broadcasted_iota(jnp.int32, (count, index.shape[1]), 0)
-    return jnp.where(places == index, 1.0, 0.0).astype(BF16)
+    places = lax.broadcasted_iota(jnp.int16, (count, index.shape[1]), 0)
+    return jnp.where(places == index.astype(jnp.int16), BF16(1), BF16(0))
 
 
 def apply_space(space, value, mesh_vel, inverse, rows):
@@ -280,11 +280,10 @@
     state[num_vars * basis :, :] = jnp.zeros((rows - num_vars * basis, elems), F32)
 
     def counted(columns, low, count):
-        places = lax.broadcasted_iota(jnp.int32, (count, chunk), 0) + low
-        total = jnp.where(places == corner_ref[0:1, columns], 1.0, 0.0)
+        total = ones_at(corner_ref[0:1, columns] - low, count)
         for i in range(1, 4):
-            total = total + jnp.where(places == corner_ref[i : i + 1, columns], 1.0, 0.0)
-        return total.astype(BF16)
+            total = total + ones_at(corner_ref[i : i + 1, columns] - low, count)
+        return total
 
     own_parts = parts[:, :verts].astype(BF16)
 

time: 65.4 us -> 59.1 us (0.904)
  Pallas kernels: 64.6 us -> 58.3 us
    pallas_call x1, Pallas kernels: 37.9 us -> 33.4 us  [body(): pl.pallas_call(functools.partial(back_kernel, (num_vars, basis, rows, tra...]
    pallas_call x1, Pallas kernels: 26.7 us -> 24.9 us  [body(): pl.pallas_call(functools.partial(front_kernel, (num_vars, basis, rows, tr...]
where the time goes in v2:
time: 59.1 us; the launch traced here: 58.9 us
  Pallas kernels  58.3 us (99%)
  between operations  0.65 us (1%)
    pallas_call x1, Pallas kernels, body(): pl.pallas_call(functools.partial(back_kernel, (num_vars, basis, rows, tra...  33.4 us
    pallas_call x1, Pallas kernels, body(): pl.pallas_call(functools.partial(front_kernel, (num_vars, basis, rows, tr...  24.9 us

profile of v2, /device:TPU:0, one launch (start us, length us, event | category | flops | bytes accessed | tf_op | source)
XLA Modules:
  0.0 58.9 jit_solution(14003971434833352764)
XLA Ops:
  0.6 24.9 %front.1 = (f32[112,2048]{1,0:T(8,128)}, f32[8,2048]{1,0:T(8,128)}, f32[8,128]{1,0:T(8,128)}, f32[80,768]{1,0:T(8,128)}, f32[80,768]{1,0:T(8,128)}, /*index=5*/b...) custom-call(f32[10,11,2048]{2,1,0:T(8,128)} %bitcast.10, ...), custom_call_target="tpu_custom_call" | custom-call | tf_op jit(solution)/shard_map/front/pallas_call | solution.py:661
  25.5 33.4 %back.1 = (f32[10,11,2048]{2,1,0:T(8,128)}, f32[1,1]{1,0:T(1,128)}) custom-call(f32[112,2048]{1,0:T(8,128)} %get-tuple-element.15.table_ref, f32[8,2048]{1,0:T(8,128)} %get-tuple-element.16.motion_ref, f32[80,768]{1,0:T(8,128)} %get-tuple-element.17.own_ref, f32[80,768]{1,0:T(8,128)} %get-tuple-element.18.theirs_ref, ...), custom_call_target="tpu_custom_call" | custom-call | tf_op jit(solution)/shard_map/back/pallas_call | solution.py:715

commit v3 on v2

--- a/solution.py
+++ b/solution.py
@@ -105,9 +105,9 @@
     found = dot(table, ones)
     high, low = found[:rows].astype(BF16), found[rows:].astype(BF16)
     every = dot(trace_op, jnp.concatenate([high, low, high], axis=0))
-    trace = jnp.where(faces == 0, every[:trace_rows], 0.0)
-    for k in range(1, num_faces):
-        trace = trace + jnp.where(faces == k, every[k * trace_rows : (k + 1) * trace_rows], 0.0)
+    trace = every[(num_faces - 1) * trace_rows :]
+    for k in range(num_faces - 1):
+        trace = jnp.where(faces == k, every[k * trace_rows : (k + 1) * trace_rows], trace)
     return trace
 
 
@@ -524,15 +524,16 @@
         return result
 
     def lifted(flux, faces, where_ones):
-        high = flux.astype(BF16).astype(F32)
-        low = flux - high
-        highs = [jnp.where(faces == k, high, 0.0).astype(BF16) for k in range(num_faces)]
-        lows = [jnp.where(faces == k, low, 0.0).astype(BF16) for k in range(num_faces)]
+        high, low = split(flux)
+        chosen = jnp.broadcast_to(faces.astype(jnp.int16), flux.shape)
+        highs = [jnp.where(chosen == k, high, BF16(0)) for k in range(num_faces)]
+        lows = [jnp.where(chosen == k, low, BF16(0)) for k in range(num_faces)]
         value = dot(lifting_ref[...], jnp.concatenate(highs + lows + highs, axis=0))
         pair = jnp.concatenate(split(value), axis=0)
-        return lax.dot_general(
+        found = lax.dot_general(
             where_ones, pair, (((1,), (1,)), ((), ())), preferred_element_type=F32
         )
+        return found[:, :lift_rows] + found[:, lift_rows:]
 
     faces = bound_index_ref[1:2, :]
     ones_bound[...] = ones_at(bound_index_ref[0:1, :], elems)
@@ -574,7 +575,7 @@
         value = apply_space(
             space_ref[...], table_ref[:, columns], motion_ref[:, columns], inverse, rows
         )
-        face_term = jnp.transpose(total[columns, :lift_rows] + total[columns, lift_rows:])
+        face_term = jnp.transpose(total[columns, :])
         rate = -(value + face_term[:rows] * inverse)
         for b in range(basis):
             rate_ref[b, :, columns] = rate[b * num_vars : (b + 1) * num_vars]
@@ -727,7 +728,7 @@
             pltpu.VMEM((2 * rows, elems), BF16),
             pltpu.VMEM((elems, 2 * tile), BF16),
             pltpu.VMEM((elems, sides), BF16),
-            pltpu.VMEM((elems, 2 * lift_rows), F32),
+            pltpu.VMEM((elems, lift_rows), F32),
         ],
         compiler_params=pltpu.CompilerParams(vmem_limit_bytes=VMEM_BYTES),
         name="back",

time: 59.1 us -> 59.4 us (level)
  no operation moved by 1% of the time
where the time goes in v3:
time: 59.4 us; the launch traced here: 59.2 us
  Pallas kernels  58.6 us (99%)
  between operations  0.65 us (1%)
    pallas_call x1, Pallas kernels, body(): pl.pallas_call(functools.partial(back_kernel, (num_vars, basis, rows, tra...  33.7 us
    pallas_call x1, Pallas kernels, body(): pl.pallas_call(functools.partial(front_kernel, (num_vars, basis, rows, tr...  24.9 us

profile of v3, /device:TPU:0, one launch (start us, length us, event | category | flops | bytes accessed | tf_op | source)
XLA Modules:
  0.0 59.2 jit_solution(8689890263120066927)
XLA Ops:
  0.6 24.9 %front.1 = (f32[112,2048]{1,0:T(8,128)}, f32[8,2048]{1,0:T(8,128)}, f32[8,128]{1,0:T(8,128)}, f32[80,768]{1,0:T(8,128)}, f32[80,768]{1,0:T(8,128)}, /*index=5*/b...) custom-call(f32[10,11,2048]{2,1,0:T(8,128)} %bitcast.10, ...), custom_call_target="tpu_custom_call" | custom-call | tf_op jit(solution)/shard_map/front/pallas_call | solution.py:662
  25.5 33.7 %back.1 = (f32[10,11,2048]{2,1,0:T(8,128)}, f32[1,1]{1,0:T(1,128)}) custom-call(f32[112,2048]{1,0:T(8,128)} %get-tuple-element.15.table_ref, f32[8,2048]{1,0:T(8,128)} %get-tuple-element.16.motion_ref, f32[80,768]{1,0:T(8,128)} %get-tuple-element.17.own_ref, f32[80,768]{1,0:T(8,128)} %get-tuple-element.18.theirs_ref, ...), custom_call_target="tpu_custom_call" | custom-call | tf_op jit(solution)/shard_map/back/pallas_call | solution.py:716
